TPU v7x, 32 devices: a whole 2x2x4 slice. The times are simulated.
32 devices in a mesh: parts: 2 (over y), tm: 8 (over z, x), band: 2 (over core).
Axes of the slice: x: 2, y: 2, z: 4, core: 2. Of those that a mesh axis runs over, the one named last changes fastest.
Arguments:
- query_tokens: bfloat16 [16, 8, 32, 2240], P(('parts', 'tm'), 'band'), parts along dimension 0, may hold values from -6 to 6
- key_tokens: bfloat16 [16, 8, 32, 2240], P(('parts', 'tm'), 'band'), parts along dimension 0, may hold values from -6 to 6
- value_tokens: bfloat16 [16, 8, 32, 2240], P(('parts', 'tm'), 'band'), parts along dimension 0, may hold values from -14 to 14
- norm_gain: float32 [2240], replicated, may hold values from 0.1 to 1.9
- out_weight: bfloat16 [2, 8, 313600], P('band', 'tm'), may hold values from -0.125 to 0.125
Outputs:
- block_out: bfloat16 [16, 8, 32, 2240], P(('parts', 'tm'), 'band'), parts along dimension 0
There are 2 independent parts, one for each index of `parts`. A program takes and returns all parts, laid end to end along the dimension named above; an argument that names none is the same for every part. Nothing has to cross between parts.
All inputs are finite; a program needn't handle non-finite values.
Results may differ from a plain program's by a relative error of at most 0.0049.
Values may be sent and summed in bfloat16 or wider, within the bound.
A program may use at most 128 MiB of HBM per device.

v0:
```python
import jax
import jax.numpy as jnp
from jax import lax
from jax.sharding import PartitionSpec as P

HEADS = 70
HD = 32


norm_epsilon = 1e-06
read_epsilon = 1e-06


def entering(x, axis, combine, identity):
    peers, place = (lax.axis_size(axis), lax.axis_index(axis))
    everything = jax.tree.map(lambda part: lax.all_gather(part, axis), x)
    start = jax.tree.map(
        lambda part, zero: jnp.broadcast_to(jnp.asarray(zero, part.dtype), part.shape), x, identity
    )

    def hop(k, before):
        reached = k < place
        new = combine(before, jax.tree.map(lambda part: part[k], everything))
        return jax.tree.map(lambda a, b: jnp.where(reached, a, b), new, before)

    return lax.fori_loop(0, peers, hop, start)


def add_pair(earlier, later):
    return (earlier[0] + later[0], earlier[1] + later[1])


def body(query_tokens, key_tokens, value_tokens, norm_gain, out_weight):
    frames, rows, width, depth = query_tokens.shape
    key_relu = jax.nn.relu(key_tokens).reshape(frames, rows * width, HEADS, HD)
    value_heads = value_tokens.reshape(frames, rows * width, HEADS, HD)
    part_state = jnp.einsum(
        "fthd,fthe->fhde", key_relu, value_heads, preferred_element_type=jnp.float32
    ).reshape(frames, HEADS, HD * HD)
    part_norm = jnp.sum(key_relu, axis=1, dtype=jnp.float32)
    state_sum, norm_sum = lax.psum((part_state, part_norm), "band")
    local_state = jnp.cumsum(state_sum, axis=0)
    local_norm = jnp.cumsum(norm_sum, axis=0)
    before = entering(
        (local_state[-1], local_norm[-1]),
        "tm",
        add_pair,
        (jnp.zeros_like(local_state[-1]), jnp.zeros_like(local_norm[-1])),
    )
    prefix_state = local_state + before[0]
    prefix_norm = local_norm + before[1]
    query_relu = jax.nn.relu(query_tokens.astype(jnp.float32)).reshape(
        frames, rows * width, HEADS, HD
    )
    numer = jnp.einsum(
        "fthd,fhde->fthe",
        query_relu,
        prefix_state.reshape(frames, HEADS, HD, HD),
        precision=lax.Precision.HIGHEST,
    )
    denom = (
        jnp.einsum("fthd,fhd->fth", query_relu, prefix_norm, precision=lax.Precision.HIGHEST)
        + read_epsilon
    )
    reads = (numer / denom[:, :, :, None]).reshape(frames * rows * width, depth)
    square = jnp.mean(reads * reads, axis=-1, keepdims=True)
    normed = (reads * lax.rsqrt(square + norm_epsilon) * norm_gain).astype(jnp.bfloat16)
    gathered = lax.all_gather(out_weight, "tm", axis=1, tiled=True)
    rows_half = gathered.reshape(-1, depth)
    result = jnp.dot(
        normed,
        lax.all_gather(rows_half, "band", axis=0, tiled=True),
        preferred_element_type=jnp.float32,
    )
    return result.astype(jnp.bfloat16).reshape(frames, rows, width, depth)


def solution(mesh):
    in_specs = (
        P(("parts", "tm"), "band", None, None),
        P(("parts", "tm"), "band", None, None),
        P(("parts", "tm"), "band", None, None),
        P(),
        P("band", "tm", None),
    )
    out_specs = P(("parts", "tm"), "band", None, None)
    return jax.shard_map(body, mesh=mesh, in_specs=in_specs, out_specs=out_specs, check_vma=False)
```

profile of v0, /device:TPU:0, one launch (start us, length us, event | category | flops | bytes accessed | tf_op | source)
XLA Modules:
  0.0 356.7 jit_solution(12308929848867415624)
XLA Ops:
  7.4 0.0 all-reduce.2.cloned.1.call-start
  7.4 1.1 broadcast_maximum_fusion
  8.5 0.0 copy-start.4
  8.5 2.0 reshape.61
  10.5 0.0 copy-done.4
  10.5 3.0 reshape.62
  13.4 2.4 fusion
  15.9 1.6 copy.32
  17.4 0.0 all-reduce.2.cloned.1.call-update
  17.5 0.0 all-gather.6.cloned.1.call-start
  17.5 0.5 all-gather.6.cloned.1.call-update
  18.0 0.0 all-gather.4.cloned.1.call-start
  18.1 21.0 %all-reduce.2.cloned.1.call-done = f32[1,70,1024]{1,2,0:T(8,128)} async-done(((f32[1,70,1024]{1,2,0:T(8,128)}), f32[1,70,1024]{1,2,0:T(8,128)}) %all-reduce.2.cloned.1.call-update) | async-done | bytes 286736 | tf_op jit(solution)/shard_map/psum | solution.py:41
  39.0 2.0 copy.33
  41.0 0.0 all-gather.4.cloned.1.call-update
  41.0 0.0 all-gather.8.cloned.1.call-start
  41.1 126.8 %all-gather.6.cloned.1.call-done = bf16[1,8,313600]{2,0,1:T(2,128)(2,1)} async-done(((bf16[1,1,313600]{2,0,1:T(2,128)(2,1)}), bf16[1,8,313600]{2,0,1:T(2,128)(2,1)}) %all-gather.6.cloned.1.call-update) | async-done | bytes 5017616 | tf_op jit(solution)/shard_map/all_gather | solution.py:68
  167.8 90.6 %reduce.3 = bf16[8,313600]{1,0:T(8,128)(2,1)} reduce(bf16[1,8,313600]{2,0,1:T(2,128)(2,1)} %all-gather.6.cloned.1.call-done, bf16[]{:T(256)} %constant.55), dimensions={0}, to_apply=%all_gather.14.reduce_sub_computation | reduce | bytes 10035202 | tf_op jit(solution)/shard_map/all_gather | solution.py:68
  258.4 12.1 %reshape.73 = bf16[2508800]{0:T(1024)(128)(2,1)} reshape(bf16[8,313600]{1,0:T(8,128)(2,1)} %reduce.3) | data formatting | bytes 10035200
  270.5 9.4 %reshape.68 = bf16[1120,2240]{1,0:T(8,128)(2,1)} reshape(bf16[2508800]{0:T(1024)(128)(2,1)} %reshape.73) | data formatting | bytes 10035200 | tf_op jit(solution)/shard_map/reshape | solution.py:69
  279.9 0.0 copy-start
  279.9 0.0 all-gather.8.cloned.1.call-update
  280.0 0.0 copy-start.3
  280.0 1.0 copy-done
  281.0 0.1 convert_reduce_fusion
  281.1 0.1 reduce_sum.21
  281.2 3.5 psum.15
  284.7 0.1 copy.34
  284.8 0.0 copy-done.3
  284.8 0.1 convert_maximum_fusion
  284.9 3.7 %reshape.65 = f32[128,70,32]{2,1,0:T(8,128)} reshape(f32[1,4,32,2240]{3,2,1,0:T(8,128)S(1)} %convert_maximum_fusion) | data formatting | bytes 2293760 | tf_op jit(solution)/shard_map/reshape.5
  288.5 4.7 %copy.38 = f32[128,70,32]{0,2,1:T(8,128)S(1)} copy(f32[128,70,32]{2,1,0:T(8,128)} %reshape.65) | data formatting | bytes 2293760 | tf_op jit(solution)/shard_map/reshape.5
  293.2 30.5 %all_gather.13 = f32[8,70,32]{1,2,0:T(8,128)S(1)} all-gather(f32[1,70,32]{1,2,0:T(8,128)S(1)} %copy.34), channel_id=1, replica_groups=mesh['parts'=2,'tm'=8,'band'=2] {'tm'}, dimensions={0}, use_global_device_ids=true | all-gather | bytes 80640 | tf_op jit(solution)/shard_map/all_gather | solution.py:16
  323.8 0.0 all-gather.4.cloned.1.call-done
  323.8 10.0 %while.16 = (s32[]{:T(128)}, f32[70,1024]{1,0:T(8,128)S(1)}, f32[70,32]{1,0:T(8,128)S(1)}, s32[]{:T(128)}, f32[8,70,1024]{2,1,0:T(8,128)}, /*index=5*/f32[8,70,32]{1,2,0:T(8,128)S(1)}, s32[]{:T(128)}, s32[]{:T(128)}) while((s32[]{:T(128)}, f32[70,1024]{1,0:T(8,128)S(1)}, f32[70,32]{1,0:T(8,128)S(1)}, s32[]{:T(128)}, ...), condition=%wide.region_4.5_spmd.clone, body=%wide.region_3.4_spmd.clone.sunk | while | flops 221764 | bytes 922995 | solution.py:26
  324.0 1.1 add_select_fusion.4
  325.1 0.1 copy.52
  325.2 1.1 add_select_fusion.4
  326.3 0.1 copy.52
  326.4 1.1 add_select_fusion.4
  327.5 0.1 copy.52
  327.6 1.1 add_select_fusion.4
  328.7 0.1 copy.52
  328.9 1.1 add_select_fusion.4
  330.0 0.1 copy.52
  330.1 1.1 add_select_fusion.4
  331.2 0.1 copy.52
  331.3 1.1 add_select_fusion.4
  332.4 0.1 copy.52
  332.5 1.1 add_select_fusion.4
  333.6 0.1 copy.52
  333.7 0.0 copy-start.1
  333.7 0.2 copy.36
  334.0 0.8 copy-done.1
  334.8 0.1 bitcast_add_fusion
  334.8 2.0 copy.37
  336.8 1.0 fusion.8
  337.8 0.2 copy-done.2
  338.1 1.5 multiply_reduce_fusion
  339.5 0.0 copy-done.5
  339.6 0.4 fusion.4
  339.9 0.0 all-gather.8.cloned.1.call-done
  340.0 8.1 %convolution_convert_fusion = bf16[128,2240]{0,1:T(8,128)(2,1)S(1)} fusion(bf16[128,2240]{0,1:T(8,128)(2,1)S(1)} %fusion.4, bf16[2240,2240]{1,0:T(8,128)(2,1)} %all-gather.8.cloned.1.call-done), kind=kOutput, calls=%fused_computation.3 | convolution fusion | flops 1284792320 | bytes 11182080 | tf_op jit(solution)/shard_map/dot_general | solution.py:70
  348.1 1.1 copy.40
  (23 shorter events, 0.2 us)
Async XLA Ops:
  7.4 31.7 %all-reduce.2.cloned.1.call-start = ((), (), s32[]{:S(2)}) async-start(), calls=%async_computation | async-start | bytes 1048576 | tf_op jit(solution)/shard_map/psum | solution.py:41
  8.5 2.0 copy-start.4
  17.5 150.4 %all-gather.6.cloned.1.call-start = ((), (), s32[]{:S(2)}) async-start(), calls=%async_computation.2 | async-start | bytes 11289600 | tf_op jit(solution)/shard_map/all_gather | solution.py:68
  18.0 305.7 %all-gather.4.cloned.1.call-start = ((), (), s32[]{:S(2)}) async-start(), calls=%async_computation.1 | async-start | bytes 2654208 | tf_op jit(solution)/shard_map/all_gather | solution.py:16
  41.0 298.9 %all-gather.8.cloned.1.call-start = ((), (), s32[]{:S(2)}) async-start(), calls=%async_computation.3 | async-start | bytes 15482880 | tf_op jit(solution)/shard_map/all_gather | solution.py:72
  279.9 1.1 copy-start
  280.0 4.8 %copy-start.3 = (bf16[1,4,32,2240]{3,2,1,0:T(8,128)(2,1)S(1)}, bf16[1,4,32,2240]{3,2,1,0:T(8,128)(2,1)}, u32[]{:S(2)}) copy-start(bf16[1,4,32,2240]{3,2,1,0:T(8,128)(2,1)} %param.7) | copy-start | bytes 1720324
  333.7 1.0 copy-start.1
  336.8 1.3 copy-start.2
  338.1 1.5 copy-start.5
Sparse Core Ops, SparseCore 0:
  17.6 21.4 all-reduce.1
Sparse Core Ops, SparseCore 1:
  20.1 147.7 all-gather.5
  170.1 49.9 all-gather.3
  280.1 20.7 all-gather.7
where the time goes:
time: 358 us; the launch traced here: 357 us
  waiting for transfers between devices  148 us (41%)
  other arithmetic  101 us (28%)
  local copies, waits for them, and re-layouts  44.6 us (12%)
  blocking collectives  34 us (9%)
  between operations  15.2 us (4%)
  matrix products  13 us (4%)
    all_gather x1, waiting for transfers between devices, body(): gathered = lax.all_gather(out_weight, 'tm', axis=1, tiled=True)  127 us
    all_gather x1, other arithmetic, body(): gathered = lax.all_gather(out_weight, 'tm', axis=1, tiled=True)  90.6 us
    all_gather x1, blocking collectives, entering(): everything = jax.tree.map(lambda part: lax.all_gather(part, axis), x)  30.5 us
    psum x1, waiting for transfers between devices, body(): state_sum, norm_sum = lax.psum((part_state, part_norm), 'band')  21 us
    unnamed x13, local copies, waits for them, and re-layouts  14.1 us
    another operation x4, local copies, waits for them, and re-layouts  13.3 us
    reshape x1, local copies, waits for them, and re-layouts, body(): rows_half = gathered.reshape(-1, depth)  9.45 us
    select_n x16, other arithmetic, hop(): return jax.tree.map(lambda a, b: jnp.where(reached, a, b), new, before)  8.63 us
  transfers between devices with their start and end apart: 4, of which 2 were waited for; matrix products, arithmetic and copies ran while one was open for 39% of the time, Pallas kernels for 0%

commit v1 on v0

v1 whole, which is shorter than its diff:
```python
import functools

import jax
import jax.numpy as jnp
from jax import lax
from jax.experimental import pallas as pl
from jax.experimental.pallas import tpu as pltpu
from jax.sharding import PartitionSpec as P

HEADS = 70
HD = 32
LANES = 128

norm_epsilon = 1e-06
read_epsilon = 1e-06
MESH = pl.DeviceIdType.MESH


def round_up(x, m):
    return -(-x // m) * m


def entering(x, axis):
    peers, place = (lax.axis_size(axis), lax.axis_index(axis))
    everything = jax.tree.map(lambda part: lax.all_gather(part, axis), x)

    def hop(k, before):
        return jax.tree.map(
            lambda a, part: jnp.where(k < place, a + part[k], a), before, everything
        )

    return lax.fori_loop(0, peers, hop, jax.tree.map(jnp.zeros_like, x))


def plain_body(query_tokens, key_tokens, value_tokens, norm_gain, out_weight):
    frames, rows, width, depth = query_tokens.shape
    key_relu = jax.nn.relu(key_tokens).reshape(frames, rows * width, HEADS, HD)
    value_heads = value_tokens.reshape(frames, rows * width, HEADS, HD)
    part_state = jnp.einsum(
        "fthd,fthe->fhde", key_relu, value_heads, preferred_element_type=jnp.float32
    ).reshape(frames, HEADS, HD * HD)
    part_norm = jnp.sum(key_relu, axis=1, dtype=jnp.float32)
    state_sum, norm_sum = lax.psum((part_state, part_norm), "band")
    local_state = jnp.cumsum(state_sum, axis=0)
    local_norm = jnp.cumsum(norm_sum, axis=0)
    before = entering((local_state[-1], local_norm[-1]), "tm")
    prefix_state = local_state + before[0]
    prefix_norm = local_norm + before[1]
    query_relu = jax.nn.relu(query_tokens.astype(jnp.float32)).reshape(
        frames, rows * width, HEADS, HD
    )
    numer = jnp.einsum(
        "fthd,fhde->fthe",
        query_relu,
        prefix_state.reshape(frames, HEADS, HD, HD),
        precision=lax.Precision.HIGHEST,
    )
    denom = (
        jnp.einsum("fthd,fhd->fth", query_relu, prefix_norm, precision=lax.Precision.HIGHEST)
        + read_epsilon
    )
    reads = (numer / denom[:, :, :, None]).reshape(frames * rows * width, depth)
    square = jnp.mean(reads * reads, axis=-1, keepdims=True)
    normed = (reads * lax.rsqrt(square + norm_epsilon) * norm_gain).astype(jnp.bfloat16)
    gathered = lax.all_gather(out_weight, "tm", axis=1, tiled=True)
    rows_half = gathered.reshape(-1, depth)
    result = jnp.dot(
        normed,
        lax.all_gather(rows_half, "band", axis=0, tiled=True),
        preferred_element_type=jnp.float32,
    )
    return result.astype(jnp.bfloat16).reshape(frames, rows, width, depth)


def kernel(
    n, shard_rows,
    q_ref, k_ref, v_ref, g_ref, w_ref, out_ref,
    state, own, band_out, band_in, hop_out, hop_in, final, reads,
    wbuf, abuf, acut, acc, res_out, res_in,
    w_local_sem, w_send, w_recv, s_send, s_recv, a_send, a_recv, r_send, r_recv,
):
    f32, bf16 = jnp.float32, jnp.bfloat16
    tokens, depth = q_ref.shape
    half = state.shape[2]
    block = wbuf.shape[2]
    hops = n.bit_length() - 1
    groups = -(-depth // LANES)
    per_half = half // LANES

    y, t, b = lax.axis_index("parts"), lax.axis_index("tm"), lax.axis_index("band")
    oy, ob = 1 - y, 1 - b
    mine = y * 2 + b

    def at(py, pt, pb):
        return {"parts": py, "tm": pt, "band": pb}

    odd = t % 2
    pos = (1 - odd) * (t // 2) + odd * (n - 1 - t // 2)

    def chip(p):
        p = lax.rem(p + 2 * n, n)
        back = p // (n // 2)
        return (1 - back) * (2 * p) + back * (2 * (n - 1 - p) + 1)

    right, left = chip(pos + 1), chip(pos - 1)

    barrier = pltpu.get_barrier_semaphore()
    peers = [at(y, t, ob), at(oy, t, b), at(oy, t, ob)]
    for side in (right, left):
        peers += [at(y, side, b), at(y, side, ob)]
    for s in range(hops):
        d = 1 << s
        peers += [at(y, lax.rem(t + d, n), b), at(y, lax.rem(t + n - d, n), b)]
    for peer in peers:
        pl.semaphore_signal(barrier, inc=1, device_id=peer, device_id_type=MESH)
    pl.semaphore_wait(barrier, len(peers))

    def remote(src, dst, send, recv, peer):
        return pltpu.make_async_remote_copy(
            src_ref=src, dst_ref=dst, send_sem=send, recv_sem=recv,
            device_id=peer, device_id_type=MESH,
        )

    def columns(pb):
        return w_ref.at[:, pl.ds(pl.multiple_of((y * 2 + pb) * block, LANES), block)]

    sends = []
    me_slot = b * n + t
    local = pltpu.make_async_copy(columns(b), wbuf.at[me_slot], w_local_sem)
    local.start()
    pair = remote(columns(ob), wbuf.at[me_slot], w_send.at[0], w_recv.at[me_slot], at(y, t, ob))
    pair.start()
    sends.append((None, pair))
    counter = [1]

    def w_put(src, slot, peer):
        copy = remote(src, wbuf.at[slot], w_send.at[counter[0]], w_recv.at[slot], peer)
        counter[0] += 1
        copy.start()
        sends.append((None, copy))

    def w_wait(slot):
        remote(wbuf.at[slot], wbuf.at[slot], w_send.at[0], w_recv.at[slot], at(y, t, ob)).wait_recv()

    if n > 2:
        for side in (right, left):
            w_put(columns(b), me_slot, at(y, side, b))
            w_put(columns(ob), me_slot, at(y, side, ob))
    arrived = []

    def forward(s):
        last = n // 2
        from_left, from_right = chip(pos - s), chip(pos + s)
        jobs = []
        if s < last:
            for beta in range(2):
                jobs += [(beta * n + from_left, right, s < last - 1 or beta == 0),
                         (beta * n + from_right, left, s < last - 1 or beta == 1)]
        else:
            jobs = [(from_left, right, False), (n + from_right, left, False)]
        for slot, side, on in jobs:
            w_wait(slot)
            if on:
                w_put(wbuf.at[slot], slot, at(y, side, b))
            arrived.append(slot)

    def pack(x):
        hi = x[HD:].astype(bf16).astype(f32)
        return jnp.concatenate([x[:HD], hi, x[HD:] - hi], axis=0).astype(bf16)

    def unpack(x):
        x = x.astype(f32)
        return jnp.concatenate([x[:HD], x[HD : HD + 8] + x[HD + 8 :]], axis=0)

    state[...] = jnp.zeros_like(state)
    ones = jnp.ones((8, tokens), bf16)
    for g in range(groups):
        lo, wide = g * LANES, min(LANES, depth - g * LANES)
        kg = jnp.maximum(k_ref[:, lo : lo + wide], 0)
        vg = v_ref[:, lo : lo + wide]
        full = lax.dot_general(kg, vg, (((0,), (0,)), ((), ())), preferred_element_type=f32)
        head = lax.broadcasted_iota(jnp.int32, (HD, wide), 1) // HD
        small = full[:HD]
        for h in range(1, wide // HD):
            small = jnp.where(head == h, full[h * HD : (h + 1) * HD], small)
        sums = jnp.dot(ones, kg, preferred_element_type=f32)
        where = pl.ds((g % per_half) * LANES, wide)
        state[g // per_half, :HD, where] = small
        state[g // per_half, HD:, where] = sums

    band_out[...] = pack(state[ob])
    swap = remote(band_out, band_in, s_send.at[0], s_recv.at[0], at(y, t, ob))
    swap.start()
    sends.append((None, swap))
    swap.wait_recv()
    own[...] = state[b] + unpack(band_in[...])

    for s in range(hops):
        d = 1 << s
        hop = remote(
            hop_out.at[s], hop_in.at[s], s_send.at[1 + s], s_recv.at[1 + s],
            at(y, lax.rem(t + d, n), b),
        )
        hop_out[s] = pack(own[...])

        @pl.when(t + d < n)
        def _():
            hop.start()

        sends.append((t + d < n, hop))

        @pl.when(t >= d)
        def _():
            hop.wait_recv()
            own[...] += unpack(hop_in[s])

    final[b] = pack(own[...])
    swap = remote(final.at[b], final.at[b], s_send.at[1 + hops], s_recv.at[1 + hops], at(y, t, ob))
    swap.start()
    sends.append((None, swap))
    if n > 2:
        forward(1)
    swap.wait_recv()

    total = jnp.zeros((tokens, 1), f32)
    for g in range(groups):
        lo, wide = g * LANES, min(LANES, depth - g * LANES)
        qg = jnp.maximum(q_ref[:, lo : lo + wide], 0)
        packed = final[g // per_half, :, pl.ds((g % per_half) * LANES, wide)]
        same = (
            lax.broadcasted_iota(jnp.int32, (wide, wide), 0) // HD
            == lax.broadcasted_iota(jnp.int32, (wide, wide), 1) // HD
        )
        small = packed.astype(f32)
        tall = jnp.concatenate([small[:HD]] * (wide // HD), axis=0)
        numer = jnp.dot(qg, jnp.where(same, tall, 0.0).astype(bf16), preferred_element_type=f32)
        weigh = small[HD : HD + 1] + small[HD + 8 : HD + 9]
        terms = qg.astype(f32) * weigh
        hi = terms.astype(bf16)
        rest = (terms - hi.astype(f32)).astype(bf16)
        block_ones = jnp.where(same, 1.0, 0.0).astype(bf16)
        denom = (
            jnp.dot(hi, block_ones, preferred_element_type=f32)
            + jnp.dot(rest, block_ones, preferred_element_type=f32)
        )
        r = numer / (denom + read_epsilon)
        reads[:, lo : lo + wide] = r
        total = total + jnp.sum(r * r, axis=-1, keepdims=True)
    scale = lax.rsqrt(total * (1.0 / depth) + norm_epsilon)
    abuf[mine] = (reads[...] * scale * g_ref[...]).astype(bf16)

    partner_slot, far_slot, far_partner = y * 2 + ob, oy * 2 + b, oy * 2 + ob

    def a_put(slot, i, peer):
        copy = remote(abuf.at[slot], abuf.at[slot], a_send.at[i], a_recv.at[slot], peer)
        copy.start()
        sends.append((None, copy))

    def a_wait(slot):
        remote(abuf.at[slot], abuf.at[slot], a_send.at[0], a_recv.at[slot], at(y, t, ob)).wait_recv()

    a_put(mine, 0, at(oy, t, b))
    a_put(mine, 1, at(y, t, ob))

    shards = 2 * n
    acut[...] = jnp.zeros_like(acut)

    def cut(slot):
        for j in range(shards):
            acut[j, slot, :, :shard_rows] = abuf[slot, :, j * shard_rows : (j + 1) * shard_rows]

    cut(mine)
    if n > 4:
        forward(2)
    a_wait(partner_slot)
    cut(partner_slot)
    a_wait(far_slot)
    a_put(far_slot, 2, at(y, t, ob))
    cut(far_slot)
    for s in range(3, n // 2):
        forward(s)
    a_wait(far_partner)
    cut(far_partner)
    local.wait()
    partner_rows = ob * n + t
    w_wait(partner_rows)

    acc[...] = jnp.zeros_like(acc)

    def add(slot):
        acc[...] += jnp.dot(
            acut[slot].reshape(4 * tokens, acut.shape[3]), wbuf[slot], preferred_element_type=f32
        )

    add(me_slot)
    add(partner_rows)
    for slot in list(arrived):
        add(slot)
    arrived.clear()
    forward(n // 2)
    for slot in arrived:
        add(slot)

    def rows_of(slot):
        return acc[pl.ds(pl.multiple_of(slot * tokens, 8), tokens), :].astype(bf16)

    for i, (slot, peer) in enumerate(
        [(far_slot, at(oy, t, b)), (far_partner, at(oy, t, ob)), (partner_slot, at(y, t, ob))]
    ):
        res_out[i] = rows_of(slot)
        copy = remote(res_out.at[i], res_in.at[mine], r_send.at[i], r_recv.at[mine], peer)
        copy.start()
        sends.append((None, copy))
    res_in[mine] = rows_of(mine)
    for slot in (partner_slot, far_slot, far_partner):
        remote(
            res_in.at[slot], res_in.at[slot], r_send.at[0], r_recv.at[slot], at(y, t, ob)
        ).wait_recv()
    for c in range(4):
        wide = min(block, depth - c * block)
        out_ref[:, c * block : c * block + wide] = res_in[c, :, :wide]
    for condition, copy in sends:
        if condition is None:
            copy.wait_send()
        else:
            pl.when(condition)(copy.wait_send)


def fast_body(n, query_tokens, key_tokens, value_tokens, norm_gain, out_weight):
    frames, rows, width, depth = query_tokens.shape
    tokens = frames * rows * width
    shard_rows = out_weight.size // depth
    padded = round_up(shard_rows, 16)
    block = round_up(-(-depth // 4), LANES)
    half = round_up(-(-depth // 2), LANES)
    hops = n.bit_length() - 1
    weight = jnp.pad(
        out_weight.reshape(shard_rows, depth),
        ((0, padded - shard_rows), (0, 4 * block - depth)),
    )
    flat = [x.reshape(tokens, depth) for x in (query_tokens, key_tokens, value_tokens)]
    f32, bf16 = jnp.float32, jnp.bfloat16
    packed = HD + 16
    dma = pltpu.SemaphoreType.DMA
    out = pl.pallas_call(
        functools.partial(kernel, n, shard_rows),
        out_shape=jax.ShapeDtypeStruct((tokens, depth), bf16),
        in_specs=[pl.BlockSpec(memory_space=pltpu.VMEM)] * 5,
        out_specs=pl.BlockSpec(memory_space=pltpu.VMEM),
        scratch_shapes=[
            pltpu.VMEM((2, HD + 8, half), f32),
            pltpu.VMEM((HD + 8, half), f32),
            pltpu.VMEM((packed, half), bf16),
            pltpu.VMEM((packed, half), bf16),
            pltpu.VMEM((hops, packed, half), bf16),
            pltpu.VMEM((hops, packed, half), bf16),
            pltpu.VMEM((2, packed, half), bf16),
            pltpu.VMEM((tokens, depth), f32),
            pltpu.VMEM((2 * n, padded, block), bf16),
            pltpu.VMEM((4, tokens, depth), bf16),
            pltpu.VMEM((2 * n, 4, tokens, padded), bf16),
            pltpu.VMEM((4 * tokens, block), f32),
            pltpu.VMEM((3, tokens, block), bf16),
            pltpu.VMEM((4, tokens, block), bf16),
            dma(()),
            dma((2 * n + 8,)),
            dma((2 * n,)),
            dma((hops + 2,)),
            dma((hops + 2,)),
            dma((3,)),
            dma((4,)),
            dma((3,)),
            dma((4,)),
        ],
        compiler_params=pltpu.CompilerParams(
            collective_id=0, has_side_effects=True, vmem_limit_bytes=48 * 1024 * 1024
        ),
    )(*flat, norm_gain.reshape(1, depth), weight)
    return out.reshape(query_tokens.shape)


def solution(mesh):
    n, bands, parts = mesh.shape["tm"], mesh.shape["band"], mesh.shape["parts"]

    def body(query_tokens, key_tokens, value_tokens, norm_gain, out_weight):
        depth = query_tokens.shape[3]
        ring = n >= 4 and n & (n - 1) == 0 and bands == 2 and parts == 2
        if ring and query_tokens.shape[0] == 1 and out_weight.size % depth == 0:
            return fast_body(n, query_tokens, key_tokens, value_tokens, norm_gain, out_weight)
        return plain_body(query_tokens, key_tokens, value_tokens, norm_gain, out_weight)

    spread = P(("parts", "tm"), "band", None, None)
    return jax.shard_map(
        body,
        mesh=mesh,
        in_specs=(spread, spread, spread, P(), P("band", "tm", None)),
        out_specs=spread,
        check_vma=False,
    )
```

time: 358 us -> 75.5 us (0.21)
  the two profiles are of different devices: /device:TPU:0 before, /device:TPU:23 now
where the time goes in v1:
time: 75.5 us; the launch traced here: 75.3 us
  Pallas kernels  59 us (78%)
  other arithmetic  14 us (19%)
  local copies, waits for them, and re-layouts  2.2 us (3%)
    pallas_call x1, Pallas kernels, fast_body(): pl.pallas_call(functools.partial(kernel, n, shard_rows), out_shape=jax.Sh...  59 us
    unnamed x1, other arithmetic  14 us

profile of v1, /device:TPU:23, one launch (start us, length us, event | category | flops | bytes accessed | tf_op | source)
XLA Modules:
  0.0 75.3 jit_solution(14956046531320911079)
XLA Ops:
  0.0 14.0 %reduce = bf16[313600]{0:T(1024)(128)(2,1)S(1)} reduce(bf16[1,1,313600]{2,1,0:T(2,128)(2,1)} %param.9, bf16[]{:T(256)} %constant.9), dimensions={0,1}, to_apply=%param.9.reduce_sub_computation | reduce | bytes 1254402 | tf_op args[4]
  14.0 0.0 copy-start.3
  14.0 0.0 copy-start
  14.1 0.0 copy-start.1
  14.1 0.0 copy-start.2
  14.1 0.7 reshape.22
  14.7 0.1 pad.4.w_ref
  14.8 0.0 copy-done.3
  14.8 0.3 copy-done
  15.1 0.2 copy-done.1
  15.3 0.2 copy-done.2
  15.5 59.0 %shard_map.55 = bf16[128,2240]{1,0:T(8,128)(2,1)S(1)} custom-call(bf16[128,2240]{1,0:T(8,128)(2,1)S(1)} %bitcast.5, bf16[128,2240]{1,0:T(8,128)(2,1)S(1)} %bitcast.6, bf16[128,2240]{1,0:T(8,128)(2,1)S(1)} %bitcast.7, f32[1,2240]{1,0:T(1,128)S(1)} %reshape.21.g_ref, bf16[144,2560]{1,0:T(8,128)(2,1)S(1)} %pad.4.w_ref), custom_call_target="tpu_custom_call" | custom-call | tf_op jit(solution)/shard_map/pallas_call | solution.py:345
  74.5 0.8 %copy.7 = bf16[1,4,32,2240]{3,2,1,0:T(8,128)(2,1)} copy(bf16[1,4,32,2240]{3,2,1,0:T(8,128)(2,1)S(1)} %bitcast.4) | data formatting | bytes 1146880
  (1 shorter events, 0.0 us)
Async XLA Ops:
  14.0 0.8 %copy-start.3 = (f32[2240]{0:T(1024)S(1)}, f32[2240]{0:T(1024)}, u32[]{:S(2)}) copy-start(f32[2240]{0:T(1024)} %param.8) | copy-start | bytes 26884
  14.0 1.1 %copy-start = (bf16[1,4,32,2240]{3,2,1,0:T(8,128)(2,1)S(1)}, bf16[1,4,32,2240]{3,2,1,0:T(8,128)(2,1)}, u32[]{:S(2)}) copy-start(bf16[1,4,32,2240]{3,2,1,0:T(8,128)(2,1)} %param.5) | copy-start | bytes 1720324
  14.1 1.2 %copy-start.1 = (bf16[1,4,32,2240]{3,2,1,0:T(8,128)(2,1)S(1)}, bf16[1,4,32,2240]{3,2,1,0:T(8,128)(2,1)}, u32[]{:S(2)}) copy-start(bf16[1,4,32,2240]{3,2,1,0:T(8,128)(2,1)} %param.6) | copy-start | bytes 1720324
  14.1 1.4 %copy-start.2 = (bf16[1,4,32,2240]{3,2,1,0:T(8,128)(2,1)S(1)}, bf16[1,4,32,2240]{3,2,1,0:T(8,128)(2,1)}, u32[]{:S(2)}) copy-start(bf16[1,4,32,2240]{3,2,1,0:T(8,128)(2,1)} %param.7) | copy-start | bytes 1720324

commit v2 on v1

--- a/solution.py
+++ b/solution.py
@@ -74,14 +74,14 @@
 
 def kernel(
     n, shard_rows,
-    q_ref, k_ref, v_ref, g_ref, w_ref, out_ref,
-    state, own, band_out, band_in, hop_out, hop_in, final, reads,
+    q_ref, k_ref, v_ref, g_ref, chunks_ref, out_ref,
+    w_wide, w_ref, state, own, band_out, band_in, hop_out, hop_in, final, reads,
     wbuf, abuf, acut, acc, res_out, res_in,
     w_local_sem, w_send, w_recv, s_send, s_recv, a_send, a_recv, r_send, r_recv,
 ):
     f32, bf16 = jnp.float32, jnp.bfloat16
     tokens, depth = q_ref.shape
-    half = state.shape[2]
+    half = state.shape[2] - LANES
     block = wbuf.shape[2]
     hops = n.bit_length() - 1
     groups = -(-depth // LANES)
@@ -113,6 +113,28 @@
         peers += [at(y, lax.rem(t + d, n), b), at(y, lax.rem(t + n - d, n), b)]
     for peer in peers:
         pl.semaphore_signal(barrier, inc=1, device_id=peer, device_id_type=MESH)
+
+    pairs, per_pair, tiles = shard_rows // 2, 2 * depth // LANES, -(-depth // LANES)
+    w_wide[...] = jnp.zeros_like(w_wide)
+    lower = lax.broadcasted_iota(jnp.int32, (pairs, LANES), 1) < LANES // 2
+
+    def chunk(j):
+        return chunks_ref[pl.ds(j, pairs, stride=per_pair), :]
+
+    middle = chunk(tiles - 1)
+    for j in range(tiles - 1):
+        w_wide[j, pl.ds(0, pairs, stride=2), :] = chunk(j)
+    w_wide[tiles - 1, pl.ds(0, pairs, stride=2), :] = jnp.where(lower, middle, 0.0)
+    turned = pltpu.roll(middle, LANES // 2, 1)
+    for j in range(tiles):
+        if j + 1 < tiles:
+            following = pltpu.roll(chunk(tiles + j), LANES // 2, 1)
+        else:
+            following = jnp.zeros_like(turned)
+        w_wide[j, pl.ds(1, pairs, stride=2), :] = jnp.where(lower, turned, following)
+        turned = following
+    for j in range(w_wide.shape[0]):
+        w_ref[:, j * LANES : (j + 1) * LANES] = w_wide[j].astype(bf16)
     pl.semaphore_wait(barrier, len(peers))
 
     def remote(src, dst, send, recv, peer):
@@ -164,13 +186,19 @@
                 w_put(wbuf.at[slot], slot, at(y, side, b))
             arrived.append(slot)
 
+    rows = HD // 2
+
     def pack(x):
-        hi = x[HD:].astype(bf16).astype(f32)
-        return jnp.concatenate([x[:HD], hi, x[HD:] - hi], axis=0).astype(bf16)
+        sums = x[:rows, half:]
+        hi = sums.astype(bf16).astype(f32)
+        both = jnp.concatenate([hi, sums - hi], axis=0)
+        return jnp.concatenate([x[:, :half], both], axis=1).astype(bf16)
 
     def unpack(x):
         x = x.astype(f32)
-        return jnp.concatenate([x[:HD], x[HD : HD + 8] + x[HD + 8 :]], axis=0)
+        sums = x[:rows, half:] + x[rows:, half:]
+        sums = jnp.concatenate([sums, jnp.zeros_like(sums)], axis=0)
+        return jnp.concatenate([x[:, :half], sums], axis=1)
 
     state[...] = jnp.zeros_like(state)
     ones = jnp.ones((8, tokens), bf16)
@@ -185,8 +213,9 @@
             small = jnp.where(head == h, full[h * HD : (h + 1) * HD], small)
         sums = jnp.dot(ones, kg, preferred_element_type=f32)
         where = pl.ds((g % per_half) * LANES, wide)
-        state[g // per_half, :HD, where] = small
-        state[g // per_half, HD:, where] = sums
+        state[g // per_half, :, where] = small
+        row = g % per_half
+        state[g // per_half, row : row + 1, half : half + wide] = sums[:1]
 
     band_out[...] = pack(state[ob])
     swap = remote(band_out, band_in, s_send.at[0], s_recv.at[0], at(y, t, ob))
@@ -208,6 +237,8 @@
             hop.start()
 
         sends.append((t + d < n, hop))
+        if s == hops - 1:
+            forward(1)
 
         @pl.when(t >= d)
         def _():
@@ -218,8 +249,6 @@
     swap = remote(final.at[b], final.at[b], s_send.at[1 + hops], s_recv.at[1 + hops], at(y, t, ob))
     swap.start()
     sends.append((None, swap))
-    if n > 2:
-        forward(1)
     swap.wait_recv()
 
     total = jnp.zeros((tokens, 1), f32)
@@ -232,9 +261,11 @@
             == lax.broadcasted_iota(jnp.int32, (wide, wide), 1) // HD
         )
         small = packed.astype(f32)
-        tall = jnp.concatenate([small[:HD]] * (wide // HD), axis=0)
+        tall = jnp.concatenate([small] * (wide // HD), axis=0)
         numer = jnp.dot(qg, jnp.where(same, tall, 0.0).astype(bf16), preferred_element_type=f32)
-        weigh = small[HD : HD + 1] + small[HD + 8 : HD + 9]
+        sums = final[g // per_half, :, half : half + wide].astype(f32)
+        row = g % per_half
+        weigh = sums[row : row + 1] + sums[rows + row : rows + row + 1]
         terms = qg.astype(f32) * weigh
         hi = terms.astype(bf16)
         rest = (terms - hi.astype(f32)).astype(bf16)
@@ -269,49 +300,54 @@
         for j in range(shards):
             acut[j, slot, :, :shard_rows] = abuf[slot, :, j * shard_rows : (j + 1) * shard_rows]
 
-    cut(mine)
     if n > 4:
         forward(2)
+    cut(mine)
     a_wait(partner_slot)
     cut(partner_slot)
+    for s in range(3, n // 2):
+        forward(s)
+    local.wait()
+    partner_rows = ob * n + t
+    w_wait(partner_rows)
+    arrived += [me_slot, partner_rows]
+    acc[...] = jnp.zeros_like(acc)
+
+    def add(slot, side):
+        both = acut[slot, pl.ds(2 * side, 2)].reshape(2 * tokens, acut.shape[3])
+        acc[side] += jnp.dot(both, wbuf[slot], preferred_element_type=f32)
+
+    for slot in arrived:
+        add(slot, y)
     a_wait(far_slot)
     a_put(far_slot, 2, at(y, t, ob))
     cut(far_slot)
-    for s in range(3, n // 2):
-        forward(s)
     a_wait(far_partner)
     cut(far_partner)
-    local.wait()
-    partner_rows = ob * n + t
-    w_wait(partner_rows)
-
-    acc[...] = jnp.zeros_like(acc)
-
-    def add(slot):
-        acc[...] += jnp.dot(
-            acut[slot].reshape(4 * tokens, acut.shape[3]), wbuf[slot], preferred_element_type=f32
-        )
-
-    add(me_slot)
-    add(partner_rows)
-    for slot in list(arrived):
-        add(slot)
+    for slot in arrived:
+        add(slot, oy)
     arrived.clear()
     forward(n // 2)
-    for slot in arrived:
-        add(slot)
-
-    def rows_of(slot):
-        return acc[pl.ds(pl.multiple_of(slot * tokens, 8), tokens), :].astype(bf16)
-
-    for i, (slot, peer) in enumerate(
-        [(far_slot, at(oy, t, b)), (far_partner, at(oy, t, ob)), (partner_slot, at(y, t, ob))]
-    ):
-        res_out[i] = rows_of(slot)
-        copy = remote(res_out.at[i], res_in.at[mine], r_send.at[i], r_recv.at[mine], peer)
+
+    def rows_of(side, pb):
+        return acc[side, pl.ds(pl.multiple_of(pb * tokens, 8), tokens), :].astype(bf16)
+
+    def give(i, side, pb):
+        res_out[i] = rows_of(side, pb)
+        copy = remote(
+            res_out.at[i], res_in.at[mine], r_send.at[i], r_recv.at[mine], at(side, t, pb)
+        )
         copy.start()
         sends.append((None, copy))
-    res_in[mine] = rows_of(mine)
+
+    for slot in arrived:
+        add(slot, oy)
+    give(0, oy, b)
+    give(1, oy, ob)
+    for slot in arrived:
+        add(slot, y)
+    give(2, y, ob)
+    res_in[mine] = rows_of(y, b)
     for slot in (partner_slot, far_slot, far_partner):
         remote(
             res_in.at[slot], res_in.at[slot], r_send.at[0], r_recv.at[slot], at(y, t, ob)
@@ -334,13 +370,10 @@
     block = round_up(-(-depth // 4), LANES)
     half = round_up(-(-depth // 2), LANES)
     hops = n.bit_length() - 1
-    weight = jnp.pad(
-        out_weight.reshape(shard_rows, depth),
-        ((0, padded - shard_rows), (0, 4 * block - depth)),
-    )
+    weight = out_weight.astype(jnp.float32).reshape(-1, LANES)
     flat = [x.reshape(tokens, depth) for x in (query_tokens, key_tokens, value_tokens)]
     f32, bf16 = jnp.float32, jnp.bfloat16
-    packed = HD + 16
+    packed = half + LANES
     dma = pltpu.SemaphoreType.DMA
     out = pl.pallas_call(
         functools.partial(kernel, n, shard_rows),
@@ -348,18 +381,20 @@
         in_specs=[pl.BlockSpec(memory_space=pltpu.VMEM)] * 5,
         out_specs=pl.BlockSpec(memory_space=pltpu.VMEM),
         scratch_shapes=[
-            pltpu.VMEM((2, HD + 8, half), f32),
-            pltpu.VMEM((HD + 8, half), f32),
-            pltpu.VMEM((packed, half), bf16),
-            pltpu.VMEM((packed, half), bf16),
-            pltpu.VMEM((hops, packed, half), bf16),
-            pltpu.VMEM((hops, packed, half), bf16),
-            pltpu.VMEM((2, packed, half), bf16),
+            pltpu.VMEM((4 * block // LANES, padded, LANES), f32),
+            pltpu.VMEM((padded, 4 * block), bf16),
+            pltpu.VMEM((2, HD, packed), f32),
+            pltpu.VMEM((HD, packed), f32),
+            pltpu.VMEM((HD, packed), bf16),
+            pltpu.VMEM((HD, packed), bf16),
+            pltpu.VMEM((hops, HD, packed), bf16),
+            pltpu.VMEM((hops, HD, packed), bf16),
+            pltpu.VMEM((2, HD, packed), bf16),
             pltpu.VMEM((tokens, depth), f32),
             pltpu.VMEM((2 * n, padded, block), bf16),
             pltpu.VMEM((4, tokens, depth), bf16),
             pltpu.VMEM((2 * n, 4, tokens, padded), bf16),
-            pltpu.VMEM((4 * tokens, block), f32),
+            pltpu.VMEM((2, 2 * tokens, block), f32),
             pltpu.VMEM((3, tokens, block), bf16),
             pltpu.VMEM((4, tokens, block), bf16),
             dma(()),
@@ -385,7 +420,9 @@
     def body(query_tokens, key_tokens, value_tokens, norm_gain, out_weight):
         depth = query_tokens.shape[3]
         ring = n >= 4 and n & (n - 1) == 0 and bands == 2 and parts == 2
-        if ring and query_tokens.shape[0] == 1 and out_weight.size % depth == 0:
+        whole_pairs = out_weight.size % (2 * depth) == 0 and depth % LANES == LANES // 2
+        few = round_up(-(-depth // 2), LANES) // LANES <= HD // 2
+        if ring and query_tokens.shape[0] == 1 and whole_pairs and few:
             return fast_body(n, query_tokens, key_tokens, value_tokens, norm_gain, out_weight)
         return plain_body(query_tokens, key_tokens, value_tokens, norm_gain, out_weight)
 

time: 75.5 us -> 70.2 us (0.930)
  the two profiles are of different devices: /device:TPU:23 before, /device:TPU:18 now
where the time goes in v2:
time: 70.2 us; the launch traced here: 70 us
  Pallas kernels  55.5 us (79%)
  other arithmetic  12.8 us (18%)
  local copies, waits for them, and re-layouts  1.55 us (2%)
    pallas_call x1, Pallas kernels, fast_body(): pl.pallas_call(functools.partial(kernel, n, shard_rows), out_shape=jax.Sh...  55.5 us
    reshape x1, other arithmetic, fast_body(): weight = out_weight.astype(jnp.float32).reshape(-1, LANES)  12.8 us

profile of v2, /device:TPU:18, one launch (start us, length us, event | category | flops | bytes accessed | tf_op | source)
XLA Modules:
  0.0 70.0 jit_solution(17829853088919916921)
XLA Ops:
  0.0 0.7 %reshape.23.g_ref = f32[1,2240]{1,0:T(1,128)S(1)} reshape(f32[2240]{0:T(1024)} %param.8) | data formatting | bytes 17920 | tf_op jit(solution)/shard_map/reshape | solution.py:413
  0.7 0.0 copy-start
  0.7 0.0 copy-start.1
  0.7 0.0 copy-start.2
  0.7 12.8 %convert_reduce_fusion = f32[313600]{0:T(1024)S(1)} fusion(bf16[1,1,313600]{2,1,0:T(2,128)(2,1)} %param.9), kind=kLoop, calls=%fused_computation | loop fusion | flops 313600 | bytes 1881600 | tf_op jit(solution)/shard_map/reshape | solution.py:373
  13.6 0.0 copy-done
  13.6 0.0 copy-done.1
  13.6 0.0 copy-done.2
  13.6 55.5 %shard_map.55 = bf16[128,2240]{1,0:T(8,128)(2,1)S(1)} custom-call(bf16[128,2240]{1,0:T(8,128)(2,1)S(1)} %bitcast.7, bf16[128,2240]{1,0:T(8,128)(2,1)S(1)} %bitcast.8, bf16[128,2240]{1,0:T(8,128)(2,1)S(1)} %bitcast.9, f32[1,2240]{1,0:T(1,128)S(1)} %reshape.23.g_ref, f32[2450,128]{1,0:T(8,128)S(1)} %bitcast.5), custom_call_target="tpu_custom_call" | custom-call | tf_op jit(solution)/shard_map/pallas_call | solution.py:378
  69.1 0.8 %copy.7 = bf16[1,4,32,2240]{3,2,1,0:T(8,128)(2,1)} copy(bf16[1,4,32,2240]{3,2,1,0:T(8,128)(2,1)S(1)} %bitcast.6) | data formatting | bytes 1146880
Async XLA Ops:
  0.7 12.9 %copy-start = (bf16[1,4,32,2240]{3,2,1,0:T(8,128)(2,1)S(1)}, bf16[1,4,32,2240]{3,2,1,0:T(8,128)(2,1)}, u32[]{:S(2)}) copy-start(bf16[1,4,32,2240]{3,2,1,0:T(8,128)(2,1)} %param.5) | copy-start | bytes 1720324
  0.7 12.9 %copy-start.1 = (bf16[1,4,32,2240]{3,2,1,0:T(8,128)(2,1)S(1)}, bf16[1,4,32,2240]{3,2,1,0:T(8,128)(2,1)}, u32[]{:S(2)}) copy-start(bf16[1,4,32,2240]{3,2,1,0:T(8,128)(2,1)} %param.6) | copy-start | bytes 1720324
  0.7 12.9 %copy-start.2 = (bf16[1,4,32,2240]{3,2,1,0:T(8,128)(2,1)S(1)}, bf16[1,4,32,2240]{3,2,1,0:T(8,128)(2,1)}, u32[]{:S(2)}) copy-start(bf16[1,4,32,2240]{3,2,1,0:T(8,128)(2,1)} %param.7) | copy-start | bytes 1720324

commit v3 on v2

--- a/solution.py
+++ b/solution.py
@@ -74,10 +74,10 @@
 
 def kernel(
     n, shard_rows,
-    q_ref, k_ref, v_ref, g_ref, chunks_ref, out_ref,
-    w_wide, w_ref, state, own, band_out, band_in, hop_out, hop_in, final, reads,
-    wbuf, abuf, acut, acc, res_out, res_in,
-    w_local_sem, w_send, w_recv, s_send, s_recv, a_send, a_recv, r_send, r_recv,
+    q_ref, k_ref, v_ref, g_ref, flat_ref, out_ref,
+    chunks_ref, w_wide, w_ref, state, own, band_out, band_in, hop_out, hop_in, final, reads,
+    wbuf, wrest, abuf, acc, res_out, res_in,
+    w_local_sem, w_send, w_recv, e_send, e_recv, s_send, s_recv, a_send, a_recv, r_send, r_recv,
 ):
     f32, bf16 = jnp.float32, jnp.bfloat16
     tokens, depth = q_ref.shape
@@ -114,6 +114,12 @@
     for peer in peers:
         pl.semaphore_signal(barrier, inc=1, device_id=peer, device_id_type=MESH)
 
+    size = flat_ref.shape[2]
+    for lo in range(0, size, 8 * LANES):
+        wide = min(8 * LANES, size - lo)
+        chunks_ref[lo // LANES : (lo + wide) // LANES, :] = (
+            flat_ref[0, :, lo : lo + wide].astype(f32).reshape(wide // LANES, LANES)
+        )
     pairs, per_pair, tiles = shard_rows // 2, 2 * depth // LANES, -(-depth // LANES)
     w_wide[...] = jnp.zeros_like(w_wide)
     lower = lax.broadcasted_iota(jnp.int32, (pairs, LANES), 1) < LANES // 2
@@ -143,31 +149,37 @@
             device_id=peer, device_id_type=MESH,
         )
 
-    def columns(pb):
-        return w_ref.at[:, pl.ds(pl.multiple_of((y * 2 + pb) * block, LANES), block)]
-
+    main = wbuf.shape[1]
     sends = []
-    me_slot = b * n + t
-    local = pltpu.make_async_copy(columns(b), wbuf.at[me_slot], w_local_sem)
-    local.start()
-    pair = remote(columns(ob), wbuf.at[me_slot], w_send.at[0], w_recv.at[me_slot], at(y, t, ob))
-    pair.start()
-    sends.append((None, pair))
-    counter = [1]
-
-    def w_put(src, slot, peer):
-        copy = remote(src, wbuf.at[slot], w_send.at[counter[0]], w_recv.at[slot], peer)
+    counter = [0]
+
+    def columns(pb, lo, size):
+        return w_ref.at[pl.ds(lo, size), pl.ds(pl.multiple_of((y * 2 + pb) * block, LANES), block)]
+
+    def w_put(sources, slot, peer):
+        i = counter[0]
         counter[0] += 1
+        for src, buf, sent, got in zip(sources, (wbuf, wrest), (w_send, e_send), (w_recv, e_recv)):
+            copy = remote(src, buf.at[slot], sent.at[i], got.at[slot], peer)
+            copy.start()
+            sends.append((None, copy))
+
+    def w_wait(slot):
+        for buf, sent, got in ((wbuf, w_send, w_recv), (wrest, e_send, e_recv)):
+            remote(buf.at[slot], buf.at[slot], sent.at[0], got.at[slot], at(y, t, ob)).wait_recv()
+
+    me_slot = 2 * t + b
+    own_rows = [(columns(pb, 0, main), columns(pb, main, wrest.shape[1])) for pb in (b, ob)]
+    for side in (right, left):
+        w_put(own_rows[0], me_slot, at(y, side, b))
+        w_put(own_rows[1], me_slot, at(y, side, ob))
+    w_put(own_rows[1], me_slot, at(y, t, ob))
+    locals_ = [
+        pltpu.make_async_copy(src, buf.at[me_slot], w_local_sem.at[i])
+        for i, (src, buf) in enumerate(zip(own_rows[0], (wbuf, wrest)))
+    ]
+    for copy in locals_:
         copy.start()
-        sends.append((None, copy))
-
-    def w_wait(slot):
-        remote(wbuf.at[slot], wbuf.at[slot], w_send.at[0], w_recv.at[slot], at(y, t, ob)).wait_recv()
-
-    if n > 2:
-        for side in (right, left):
-            w_put(columns(b), me_slot, at(y, side, b))
-            w_put(columns(ob), me_slot, at(y, side, ob))
     arrived = []
 
     def forward(s):
@@ -176,15 +188,16 @@
         jobs = []
         if s < last:
             for beta in range(2):
-                jobs += [(beta * n + from_left, right, s < last - 1 or beta == 0),
-                         (beta * n + from_right, left, s < last - 1 or beta == 1)]
+                jobs += [(2 * from_left + beta, right, s < last - 1 or beta == 0),
+                         (2 * from_right + beta, left, s < last - 1 or beta == 1)]
+            arrived.extend([from_left, from_right])
         else:
-            jobs = [(from_left, right, False), (n + from_right, left, False)]
+            jobs = [(2 * from_left, right, False), (2 * from_right + 1, left, False)]
+            arrived.append(from_left)
         for slot, side, on in jobs:
             w_wait(slot)
             if on:
-                w_put(wbuf.at[slot], slot, at(y, side, b))
-            arrived.append(slot)
+                w_put((wbuf.at[slot], wrest.at[slot]), slot, at(y, side, b))
 
     rows = HD // 2
 
@@ -278,7 +291,17 @@
         reads[:, lo : lo + wide] = r
         total = total + jnp.sum(r * r, axis=-1, keepdims=True)
     scale = lax.rsqrt(total * (1.0 / depth) + norm_epsilon)
-    abuf[mine] = (reads[...] * scale * g_ref[...]).astype(bf16)
+    normed = reads[...] * scale * g_ref[...][None, :]
+    shards, few = 2 * n, shard_rows - main
+    gap = jnp.zeros((tokens, wrest.shape[1] - few), f32)
+    extra = []
+    for j in range(shards):
+        slot, lo = 2 * (j % n) + j // n, j * shard_rows
+        abuf[mine, :, slot * main : (slot + 1) * main] = normed[:, lo : lo + main].astype(bf16)
+    for slot in range(shards):
+        lo = (slot % 2 * n + slot // 2) * shard_rows + main
+        extra += [normed[:, lo : lo + few], gap]
+    abuf[mine, :, shards * main :] = jnp.concatenate(extra, axis=1).astype(bf16)
 
     partner_slot, far_slot, far_partner = y * 2 + ob, oy * 2 + b, oy * 2 + ob
 
@@ -293,39 +316,35 @@
     a_put(mine, 0, at(oy, t, b))
     a_put(mine, 1, at(y, t, ob))
 
-    shards = 2 * n
-    acut[...] = jnp.zeros_like(acut)
-
-    def cut(slot):
-        for j in range(shards):
-            acut[j, slot, :, :shard_rows] = abuf[slot, :, j * shard_rows : (j + 1) * shard_rows]
-
     if n > 4:
         forward(2)
-    cut(mine)
+    acc[...] = jnp.zeros_like(acc)
     a_wait(partner_slot)
-    cut(partner_slot)
     for s in range(3, n // 2):
         forward(s)
-    local.wait()
-    partner_rows = ob * n + t
-    w_wait(partner_rows)
-    arrived += [me_slot, partner_rows]
-    acc[...] = jnp.zeros_like(acc)
-
-    def add(slot, side):
-        both = acut[slot, pl.ds(2 * side, 2)].reshape(2 * tokens, acut.shape[3])
-        acc[side] += jnp.dot(both, wbuf[slot], preferred_element_type=f32)
-
-    for slot in arrived:
-        add(slot, y)
+    for copy in locals_:
+        copy.wait()
+    w_wait(2 * t + ob)
+    arrived.append(t)
+
+    def add(p, side):
+        lanes = pl.ds(pl.multiple_of(p * 2 * main, LANES), 2 * main)
+        both = abuf[pl.ds(2 * side, 2), :, lanes].reshape(2 * tokens, 2 * main)
+        rows = wbuf[pl.ds(2 * p, 2)].reshape(2 * main, block)
+        acc[side] += jnp.dot(both, rows, preferred_element_type=f32)
+
+    def add_rest(side):
+        both = abuf[pl.ds(2 * side, 2), :, shards * main :].reshape(2 * tokens, -1)
+        rows = wrest[...].reshape(-1, block)
+        acc[side] += jnp.dot(both, rows, preferred_element_type=f32)
+
+    for p in arrived:
+        add(p, y)
     a_wait(far_slot)
     a_put(far_slot, 2, at(y, t, ob))
-    cut(far_slot)
     a_wait(far_partner)
-    cut(far_partner)
-    for slot in arrived:
-        add(slot, oy)
+    for p in arrived:
+        add(p, oy)
     arrived.clear()
     forward(n // 2)
 
@@ -340,12 +359,12 @@
         copy.start()
         sends.append((None, copy))
 
-    for slot in arrived:
-        add(slot, oy)
+    add(arrived[0], oy)
+    add_rest(oy)
     give(0, oy, b)
     give(1, oy, ob)
-    for slot in arrived:
-        add(slot, y)
+    add(arrived[0], y)
+    add_rest(y)
     give(2, y, ob)
     res_in[mine] = rows_of(y, b)
     for slot in (partner_slot, far_slot, far_partner):
@@ -370,7 +389,8 @@
     block = round_up(-(-depth // 4), LANES)
     half = round_up(-(-depth // 2), LANES)
     hops = n.bit_length() - 1
-    weight = out_weight.astype(jnp.float32).reshape(-1, LANES)
+    main = shard_rows // LANES * LANES
+    rest = padded - main
     flat = [x.reshape(tokens, depth) for x in (query_tokens, key_tokens, value_tokens)]
     f32, bf16 = jnp.float32, jnp.bfloat16
     packed = half + LANES
@@ -381,6 +401,7 @@
         in_specs=[pl.BlockSpec(memory_space=pltpu.VMEM)] * 5,
         out_specs=pl.BlockSpec(memory_space=pltpu.VMEM),
         scratch_shapes=[
+            pltpu.VMEM((out_weight.size // LANES, LANES), f32),
             pltpu.VMEM((4 * block // LANES, padded, LANES), f32),
             pltpu.VMEM((padded, 4 * block), bf16),
             pltpu.VMEM((2, HD, packed), f32),
@@ -391,13 +412,15 @@
             pltpu.VMEM((hops, HD, packed), bf16),
             pltpu.VMEM((2, HD, packed), bf16),
             pltpu.VMEM((tokens, depth), f32),
-            pltpu.VMEM((2 * n, padded, block), bf16),
-            pltpu.VMEM((4, tokens, depth), bf16),
-            pltpu.VMEM((2 * n, 4, tokens, padded), bf16),
+            pltpu.VMEM((2 * n, main, block), bf16),
+            pltpu.VMEM((2 * n, rest, block), bf16),
+            pltpu.VMEM((4, tokens, 2 * n * padded), bf16),
             pltpu.VMEM((2, 2 * tokens, block), f32),
             pltpu.VMEM((3, tokens, block), bf16),
             pltpu.VMEM((4, tokens, block), bf16),
-            dma(()),
+            dma((2,)),
+            dma((2 * n + 8,)),
+            dma((2 * n,)),
             dma((2 * n + 8,)),
             dma((2 * n,)),
             dma((hops + 2,)),
@@ -410,7 +433,7 @@
         compiler_params=pltpu.CompilerParams(
             collective_id=0, has_side_effects=True, vmem_limit_bytes=48 * 1024 * 1024
         ),
-    )(*flat, norm_gain.reshape(1, depth), weight)
+    )(*flat, norm_gain, out_weight)
     return out.reshape(query_tokens.shape)
 
 
@@ -422,6 +445,7 @@
         ring = n >= 4 and n & (n - 1) == 0 and bands == 2 and parts == 2
         whole_pairs = out_weight.size % (2 * depth) == 0 and depth % LANES == LANES // 2
         few = round_up(-(-depth // 2), LANES) // LANES <= HD // 2
+        ring = ring and LANES < out_weight.size // depth
         if ring and query_tokens.shape[0] == 1 and whole_pairs and few:
             return fast_body(n, query_tokens, key_tokens, value_tokens, norm_gain, out_weight)
         return plain_body(query_tokens, key_tokens, value_tokens, norm_gain, out_weight)

time: 70.2 us -> 58.7 us (0.84)
  the two profiles are of different devices: /device:TPU:18 before, /device:TPU:31 now
where the time goes in v3:
time: 58.7 us; the launch traced here: 58.3 us
  Pallas kernels  52.3 us (89%)
  local copies, waits for them, and re-layouts  6.01 us (10%)
    pallas_call x1, Pallas kernels, fast_body(): pl.pallas_call(functools.partial(kernel, n, shard_rows), out_shape=jax.Sh...  52.3 us
    unnamed x11, local copies, waits for them, and re-layouts  6.01 us

profile of v3, /device:TPU:31, one launch (start us, length us, event | category | flops | bytes accessed | tf_op | source)
XLA Modules:
  0.0 58.3 jit_solution(16890584372266131379)
XLA Ops:
  0.0 0.0 copy-start
  0.0 1.3 %copy-done = bf16[1,1,313600]{2,1,0:T(2,128)(2,1)S(1)} copy-done((bf16[1,1,313600]{2,1,0:T(2,128)(2,1)S(1)}, bf16[1,1,313600]{2,1,0:T(2,128)(2,1)}, u32[]{:S(2)}) %copy-start) | copy-done | bytes 627224
  1.3 0.0 copy-start.1
  1.3 1.1 %copy-done.1 = bf16[1,4,32,2240]{3,2,1,0:T(8,128)(2,1)S(1)} copy-done((bf16[1,4,32,2240]{3,2,1,0:T(8,128)(2,1)S(1)}, bf16[1,4,32,2240]{3,2,1,0:T(8,128)(2,1)}, u32[]{:S(2)}) %copy-start.1) | copy-done | bytes 573464
  2.4 0.0 copy-start.2
  2.4 1.1 %copy-done.2 = bf16[1,4,32,2240]{3,2,1,0:T(8,128)(2,1)S(1)} copy-done((bf16[1,4,32,2240]{3,2,1,0:T(8,128)(2,1)S(1)}, bf16[1,4,32,2240]{3,2,1,0:T(8,128)(2,1)}, u32[]{:S(2)}) %copy-start.2) | copy-done | bytes 573464
  3.4 0.0 copy-start.3
  3.4 1.1 %copy-done.3 = bf16[1,4,32,2240]{3,2,1,0:T(8,128)(2,1)S(1)} copy-done((bf16[1,4,32,2240]{3,2,1,0:T(8,128)(2,1)S(1)}, bf16[1,4,32,2240]{3,2,1,0:T(8,128)(2,1)}, u32[]{:S(2)}) %copy-start.3) | copy-done | bytes 573464
  4.5 0.0 copy-start.4
  4.5 0.7 %copy-done.4 = f32[2240]{0:T(1024)S(1)} copy-done((f32[2240]{0:T(1024)S(1)}, f32[2240]{0:T(1024)}, u32[]{:S(2)}) %copy-start.4) | copy-done | bytes 8984
  5.2 52.3 %shard_map.55 = bf16[128,2240]{1,0:T(8,128)(2,1)S(1)} custom-call(bf16[128,2240]{1,0:T(8,128)(2,1)S(1)} %bitcast.5, bf16[128,2240]{1,0:T(8,128)(2,1)S(1)} %bitcast.6, bf16[128,2240]{1,0:T(8,128)(2,1)S(1)} %bitcast.7, f32[2240]{0:T(1024)S(1)} %copy-done.4, bf16[1,1,313600]{2,1,0:T(2,128)(2,1)S(1)} %copy-done), custom_call_target="tpu_custom_call" | custom-call | tf_op jit(solution)/shard_map/pallas_call | solution.py:398
  57.5 0.8 %copy.7 = bf16[1,4,32,2240]{3,2,1,0:T(8,128)(2,1)} copy(bf16[1,4,32,2240]{3,2,1,0:T(8,128)(2,1)S(1)} %bitcast.4) | data formatting | bytes 1146880
Async XLA Ops:
  0.0 1.3 %copy-start = (bf16[1,1,313600]{2,1,0:T(2,128)(2,1)S(1)}, bf16[1,1,313600]{2,1,0:T(2,128)(2,1)}, u32[]{:S(2)}) copy-start(bf16[1,1,313600]{2,1,0:T(2,128)(2,1)} %flat_ref.1) | copy-start | bytes 1881604
  1.3 1.1 %copy-start.1 = (bf16[1,4,32,2240]{3,2,1,0:T(8,128)(2,1)S(1)}, bf16[1,4,32,2240]{3,2,1,0:T(8,128)(2,1)}, u32[]{:S(2)}) copy-start(bf16[1,4,32,2240]{3,2,1,0:T(8,128)(2,1)} %param.5) | copy-start | bytes 1720324
  2.4 1.1 %copy-start.2 = (bf16[1,4,32,2240]{3,2,1,0:T(8,128)(2,1)S(1)}, bf16[1,4,32,2240]{3,2,1,0:T(8,128)(2,1)}, u32[]{:S(2)}) copy-start(bf16[1,4,32,2240]{3,2,1,0:T(8,128)(2,1)} %param.6) | copy-start | bytes 1720324
  3.4 1.1 %copy-start.3 = (bf16[1,4,32,2240]{3,2,1,0:T(8,128)(2,1)S(1)}, bf16[1,4,32,2240]{3,2,1,0:T(8,128)(2,1)}, u32[]{:S(2)}) copy-start(bf16[1,4,32,2240]{3,2,1,0:T(8,128)(2,1)} %param.7) | copy-start | bytes 1720324
  4.5 0.7 %copy-start.4 = (f32[2240]{0:T(1024)S(1)}, f32[2240]{0:T(1024)}, u32[]{:S(2)}) copy-start(f32[2240]{0:T(1024)} %g_ref.1) | copy-start | bytes 26884

commit v4 on v3

--- a/solution.py
+++ b/solution.py
@@ -18,6 +18,13 @@
 
 def round_up(x, m):
     return -(-x // m) * m
+
+
+def core_widths(depth):
+    tiles = -(-depth // LANES)
+    chip = -(-tiles // 2)
+    first = -(-chip // 2)
+    return first * LANES, (chip - first) * LANES
 
 
 def entering(x, axis):
@@ -74,8 +81,8 @@
 
 def kernel(
     n, shard_rows,
-    q_ref, k_ref, v_ref, g_ref, flat_ref, out_ref,
-    chunks_ref, w_wide, w_ref, state, own, band_out, band_in, hop_out, hop_in, final, reads,
+    q_hbm, k_hbm, v_hbm, g_hbm, flat_hbm, out_ref,
+    q_ref, k_ref, v_ref, g_ref, flat_ref, in_sem, chunks_ref, w_wide, w_ref, state, own, band_out, band_in, hop_out, hop_in, final, reads,
     wbuf, wrest, abuf, acc, res_out, res_in,
     w_local_sem, w_send, w_recv, e_send, e_recv, s_send, s_recv, a_send, a_recv, r_send, r_recv,
 ):
@@ -83,9 +90,19 @@
     tokens, depth = q_ref.shape
     half = state.shape[2] - LANES
     block = wbuf.shape[2]
+    widths = core_widths(depth)
     hops = n.bit_length() - 1
     groups = -(-depth // LANES)
     per_half = half // LANES
+
+    loads = [
+        pltpu.make_async_copy(src, dst, in_sem.at[i])
+        for i, (src, dst) in enumerate(
+            [(flat_hbm, flat_ref), (k_hbm, k_ref), (v_hbm, v_ref), (q_hbm, q_ref), (g_hbm, g_ref)]
+        )
+    ]
+    for load in loads:
+        load.start()
 
     y, t, b = lax.axis_index("parts"), lax.axis_index("tm"), lax.axis_index("band")
     oy, ob = 1 - y, 1 - b
@@ -114,6 +131,7 @@
     for peer in peers:
         pl.semaphore_signal(barrier, inc=1, device_id=peer, device_id_type=MESH)
 
+    loads[0].wait()
     size = flat_ref.shape[2]
     for lo in range(0, size, 8 * LANES):
         wide = min(8 * LANES, size - lo)
@@ -153,51 +171,66 @@
     sends = []
     counter = [0]
 
-    def columns(pb, lo, size):
-        return w_ref.at[pl.ds(lo, size), pl.ds(pl.multiple_of((y * 2 + pb) * block, LANES), block)]
-
-    def w_put(sources, slot, peer):
+    def columns(core, lo, size):
+        start = pl.multiple_of(y * sum(widths) + core * widths[0], LANES)
+        return w_ref.at[pl.ds(lo, size), pl.ds(start, widths[core])]
+
+    def own_rows(core):
+        return columns(core, 0, main), columns(core, main, wrest.shape[1])
+
+    def held(slot):
+        def at_width(core):
+            return [buf.at[slot, :, pl.ds(0, widths[core])] for buf in (wbuf, wrest)]
+
+        return at_width
+
+    weight_sems = list(zip((w_send, e_send), (w_recv, e_recv)))
+
+    def w_put(sources, slot, side, pb):
         i = counter[0]
         counter[0] += 1
-        for src, buf, sent, got in zip(sources, (wbuf, wrest), (w_send, e_send), (w_recv, e_recv)):
-            copy = remote(src, buf.at[slot], sent.at[i], got.at[slot], peer)
-            copy.start()
-            sends.append((None, copy))
+        for core in range(2):
+            for src, dst, (sent, got) in zip(sources(core), held(slot)(core), weight_sems):
+                copy = remote(src, dst, sent.at[i], got.at[slot], at(y, side, pb))
+                pl.when(pb == core)(copy.start)
+                sends.append((pb == core, copy))
 
     def w_wait(slot):
-        for buf, sent, got in ((wbuf, w_send, w_recv), (wrest, e_send, e_recv)):
-            remote(buf.at[slot], buf.at[slot], sent.at[0], got.at[slot], at(y, t, ob)).wait_recv()
+        for core in range(2):
+            for dst, (sent, got) in zip(held(slot)(core), weight_sems):
+                copy = remote(dst, dst, sent.at[0], got.at[slot], at(y, t, ob))
+                pl.when(b == core)(copy.wait_recv)
 
     me_slot = 2 * t + b
-    own_rows = [(columns(pb, 0, main), columns(pb, main, wrest.shape[1])) for pb in (b, ob)]
     for side in (right, left):
-        w_put(own_rows[0], me_slot, at(y, side, b))
-        w_put(own_rows[1], me_slot, at(y, side, ob))
-    w_put(own_rows[1], me_slot, at(y, t, ob))
-    locals_ = [
-        pltpu.make_async_copy(src, buf.at[me_slot], w_local_sem.at[i])
-        for i, (src, buf) in enumerate(zip(own_rows[0], (wbuf, wrest)))
-    ]
-    for copy in locals_:
-        copy.start()
+        w_put(own_rows, me_slot, side, b)
+        w_put(own_rows, me_slot, side, ob)
+    w_put(own_rows, me_slot, t, ob)
+    locals_ = []
+    for core in range(2):
+        for i, (src, dst) in enumerate(zip(own_rows(core), held(me_slot)(core))):
+            copy = pltpu.make_async_copy(src, dst, w_local_sem.at[i])
+            pl.when(b == core)(copy.start)
+            locals_.append((b == core, copy))
     arrived = []
 
-    def forward(s):
+    def forward(s, bands=(0, 1)):
         last = n // 2
         from_left, from_right = chip(pos - s), chip(pos + s)
         jobs = []
         if s < last:
-            for beta in range(2):
+            for beta in bands:
                 jobs += [(2 * from_left + beta, right, s < last - 1 or beta == 0),
                          (2 * from_right + beta, left, s < last - 1 or beta == 1)]
-            arrived.extend([from_left, from_right])
+            if bands[-1]:
+                arrived.extend([from_left, from_right])
         else:
             jobs = [(2 * from_left, right, False), (2 * from_right + 1, left, False)]
             arrived.append(from_left)
         for slot, side, on in jobs:
             w_wait(slot)
             if on:
-                w_put((wbuf.at[slot], wrest.at[slot]), slot, at(y, side, b))
+                w_put(held(slot), slot, side, b)
 
     rows = HD // 2
 
@@ -213,6 +246,8 @@
         sums = jnp.concatenate([sums, jnp.zeros_like(sums)], axis=0)
         return jnp.concatenate([x[:, :half], sums], axis=1)
 
+    loads[1].wait()
+    loads[2].wait()
     state[...] = jnp.zeros_like(state)
     ones = jnp.ones((8, tokens), bf16)
     for g in range(groups):
@@ -250,8 +285,8 @@
             hop.start()
 
         sends.append((t + d < n, hop))
-        if s == hops - 1:
-            forward(1)
+        if s >= hops - 2:
+            forward(1, (s - hops + 2,))
 
         @pl.when(t >= d)
         def _():
@@ -264,6 +299,8 @@
     sends.append((None, swap))
     swap.wait_recv()
 
+    loads[3].wait()
+    loads[4].wait()
     total = jnp.zeros((tokens, 1), f32)
     for g in range(groups):
         lo, wide = g * LANES, min(LANES, depth - g * LANES)
@@ -322,8 +359,8 @@
     a_wait(partner_slot)
     for s in range(3, n // 2):
         forward(s)
-    for copy in locals_:
-        copy.wait()
+    for condition, copy in locals_:
+        pl.when(condition)(copy.wait)
     w_wait(2 * t + ob)
     arrived.append(t)
 
@@ -353,11 +390,18 @@
 
     def give(i, side, pb):
         res_out[i] = rows_of(side, pb)
-        copy = remote(
-            res_out.at[i], res_in.at[mine], r_send.at[i], r_recv.at[mine], at(side, t, pb)
-        )
-        copy.start()
-        sends.append((None, copy))
+        for core in range(2):
+            lanes = pl.ds(0, widths[core])
+            copy = remote(
+                res_out.at[i, :, lanes], res_in.at[mine, :, lanes],
+                r_send.at[i], r_recv.at[mine], at(side, t, pb),
+            )
+            pl.when(b == core)(copy.start)
+            sends.append((b == core, copy))
+
+    def take(slot, core):
+        view = res_in.at[slot, :, pl.ds(0, widths[core])]
+        remote(view, view, r_send.at[0], r_recv.at[slot], at(y, t, ob)).wait_recv()
 
     add(arrived[0], oy)
     add_rest(oy)
@@ -367,13 +411,13 @@
     add_rest(y)
     give(2, y, ob)
     res_in[mine] = rows_of(y, b)
-    for slot in (partner_slot, far_slot, far_partner):
-        remote(
-            res_in.at[slot], res_in.at[slot], r_send.at[0], r_recv.at[slot], at(y, t, ob)
-        ).wait_recv()
+    for slot, pb in ((partner_slot, ob), (far_slot, b), (far_partner, ob)):
+        for core in range(2):
+            pl.when(pb == core)(functools.partial(take, slot, core))
     for c in range(4):
-        wide = min(block, depth - c * block)
-        out_ref[:, c * block : c * block + wide] = res_in[c, :, :wide]
+        start = c // 2 * sum(widths) + c % 2 * widths[0]
+        wide = min(widths[c % 2], depth - start)
+        out_ref[:, start : start + wide] = res_in[c, :, :wide]
     for condition, copy in sends:
         if condition is None:
             copy.wait_send()
@@ -386,11 +430,12 @@
     tokens = frames * rows * width
     shard_rows = out_weight.size // depth
     padded = round_up(shard_rows, 16)
-    block = round_up(-(-depth // 4), LANES)
+    block = core_widths(depth)[0]
     half = round_up(-(-depth // 2), LANES)
     hops = n.bit_length() - 1
     main = shard_rows // LANES * LANES
     rest = padded - main
+    wide = 2 * sum(core_widths(depth))
     flat = [x.reshape(tokens, depth) for x in (query_tokens, key_tokens, value_tokens)]
     f32, bf16 = jnp.float32, jnp.bfloat16
     packed = half + LANES
@@ -398,12 +443,16 @@
     out = pl.pallas_call(
         functools.partial(kernel, n, shard_rows),
         out_shape=jax.ShapeDtypeStruct((tokens, depth), bf16),
-        in_specs=[pl.BlockSpec(memory_space=pltpu.VMEM)] * 5,
+        in_specs=[pl.BlockSpec(memory_space=pltpu.HBM)] * 5,
         out_specs=pl.BlockSpec(memory_space=pltpu.VMEM),
         scratch_shapes=[
+            *[pltpu.VMEM((tokens, depth), bf16)] * 3,
+            pltpu.VMEM((depth,), f32),
+            pltpu.VMEM(out_weight.shape, bf16),
+            dma((5,)),
             pltpu.VMEM((out_weight.size // LANES, LANES), f32),
-            pltpu.VMEM((4 * block // LANES, padded, LANES), f32),
-            pltpu.VMEM((padded, 4 * block), bf16),
+            pltpu.VMEM((wide // LANES, padded, LANES), f32),
+            pltpu.VMEM((padded, wide), bf16),
             pltpu.VMEM((2, HD, packed), f32),
             pltpu.VMEM((HD, packed), f32),
             pltpu.VMEM((HD, packed), bf16),
@@ -431,7 +480,7 @@
             dma((4,)),
         ],
         compiler_params=pltpu.CompilerParams(
-            collective_id=0, has_side_effects=True, vmem_limit_bytes=48 * 1024 * 1024
+            collective_id=0, has_side_effects=True, vmem_limit_bytes=63 * 1024 * 1024
         ),
     )(*flat, norm_gain, out_weight)
     return out.reshape(query_tokens.shape)

time: 58.7 us -> 56.9 us (0.969)
  the two profiles are of different devices: /device:TPU:31 before, /device:TPU:29 now
where the time goes in v4:
time: 56.9 us; the launch traced here: 56.8 us
  Pallas kernels  54.8 us (96%)
  local copies, waits for them, and re-layouts  1.92 us (3%)
    pallas_call x1, Pallas kernels, fast_body(): pl.pallas_call(functools.partial(kernel, n, shard_rows), out_shape=jax.Sh...  54.8 us
    unnamed x1, local copies, waits for them, and re-layouts  1.92 us

profile of v4, /device:TPU:29, one launch (start us, length us, event | category | flops | bytes accessed | tf_op | source)
XLA Modules:
  0.0 56.8 jit_solution(10647941544191806725)
XLA Ops:
  0.0 54.8 %shard_map.55 = bf16[128,2240]{1,0:T(8,128)(2,1)} custom-call(bf16[128,2240]{1,0:T(8,128)(2,1)} %bitcast.5, bf16[128,2240]{1,0:T(8,128)(2,1)} %bitcast.6, bf16[128,2240]{1,0:T(8,128)(2,1)} %bitcast.7, f32[2240]{0:T(1024)} %g_hbm.1, bf16[1,1,313600]{2,1,0:T(2,128)(2,1)} %flat_hbm.1), custom_call_target="tpu_custom_call" | custom-call | tf_op jit(solution)/shard_map/pallas_call | solution.py:443
  54.8 1.9 %copy.7 = bf16[1,4,32,2240]{3,2,1,0:T(8,128)(2,1)} copy(bf16[1,4,32,2240]{3,2,1,0:T(8,128)(2,1)} %bitcast.4) | data formatting | bytes 1146880

commit v5 on v4

--- a/solution.py
+++ b/solution.py
@@ -98,7 +98,7 @@
     loads = [
         pltpu.make_async_copy(src, dst, in_sem.at[i])
         for i, (src, dst) in enumerate(
-            [(flat_hbm, flat_ref), (k_hbm, k_ref), (v_hbm, v_ref), (q_hbm, q_ref), (g_hbm, g_ref)]
+            [(k_hbm, k_ref), (v_hbm, v_ref), (flat_hbm, flat_ref), (q_hbm, q_ref), (g_hbm, g_ref)]
         )
     ]
     for load in loads:
@@ -131,34 +131,6 @@
     for peer in peers:
         pl.semaphore_signal(barrier, inc=1, device_id=peer, device_id_type=MESH)
 
-    loads[0].wait()
-    size = flat_ref.shape[2]
-    for lo in range(0, size, 8 * LANES):
-        wide = min(8 * LANES, size - lo)
-        chunks_ref[lo // LANES : (lo + wide) // LANES, :] = (
-            flat_ref[0, :, lo : lo + wide].astype(f32).reshape(wide // LANES, LANES)
-        )
-    pairs, per_pair, tiles = shard_rows // 2, 2 * depth // LANES, -(-depth // LANES)
-    w_wide[...] = jnp.zeros_like(w_wide)
-    lower = lax.broadcasted_iota(jnp.int32, (pairs, LANES), 1) < LANES // 2
-
-    def chunk(j):
-        return chunks_ref[pl.ds(j, pairs, stride=per_pair), :]
-
-    middle = chunk(tiles - 1)
-    for j in range(tiles - 1):
-        w_wide[j, pl.ds(0, pairs, stride=2), :] = chunk(j)
-    w_wide[tiles - 1, pl.ds(0, pairs, stride=2), :] = jnp.where(lower, middle, 0.0)
-    turned = pltpu.roll(middle, LANES // 2, 1)
-    for j in range(tiles):
-        if j + 1 < tiles:
-            following = pltpu.roll(chunk(tiles + j), LANES // 2, 1)
-        else:
-            following = jnp.zeros_like(turned)
-        w_wide[j, pl.ds(1, pairs, stride=2), :] = jnp.where(lower, turned, following)
-        turned = following
-    for j in range(w_wide.shape[0]):
-        w_ref[:, j * LANES : (j + 1) * LANES] = w_wide[j].astype(bf16)
     pl.semaphore_wait(barrier, len(peers))
 
     def remote(src, dst, send, recv, peer):
@@ -202,16 +174,16 @@
                 pl.when(b == core)(copy.wait_recv)
 
     me_slot = 2 * t + b
-    for side in (right, left):
-        w_put(own_rows, me_slot, side, b)
-        w_put(own_rows, me_slot, side, ob)
-    w_put(own_rows, me_slot, t, ob)
-    locals_ = []
-    for core in range(2):
-        for i, (src, dst) in enumerate(zip(own_rows(core), held(me_slot)(core))):
-            copy = pltpu.make_async_copy(src, dst, w_local_sem.at[i])
-            pl.when(b == core)(copy.start)
-            locals_.append((b == core, copy))
+    locals_ = [
+        (b == core, pltpu.make_async_copy(src, dst, w_local_sem.at[i]))
+        for core in range(2)
+        for i, (src, dst) in enumerate(zip(own_rows(core), held(me_slot)(core)))
+    ]
+
+    def first_step(pb):
+        for side in (right, left):
+            w_put(own_rows, me_slot, side, pb)
+
     arrived = []
 
     def forward(s, bands=(0, 1)):
@@ -222,7 +194,7 @@
             for beta in bands:
                 jobs += [(2 * from_left + beta, right, s < last - 1 or beta == 0),
                          (2 * from_right + beta, left, s < last - 1 or beta == 1)]
-            if bands[-1]:
+            if len(bands) == 2:
                 arrived.extend([from_left, from_right])
         else:
             jobs = [(2 * from_left, right, False), (2 * from_right + 1, left, False)]
@@ -246,8 +218,8 @@
         sums = jnp.concatenate([sums, jnp.zeros_like(sums)], axis=0)
         return jnp.concatenate([x[:, :half], sums], axis=1)
 
+    loads[0].wait()
     loads[1].wait()
-    loads[2].wait()
     state[...] = jnp.zeros_like(state)
     ones = jnp.ones((8, tokens), bf16)
     for g in range(groups):
@@ -269,6 +241,37 @@
     swap = remote(band_out, band_in, s_send.at[0], s_recv.at[0], at(y, t, ob))
     swap.start()
     sends.append((None, swap))
+
+    loads[2].wait()
+    size = flat_ref.shape[2]
+    for lo in range(0, size, 8 * LANES):
+        wide = min(8 * LANES, size - lo)
+        chunks_ref[lo // LANES : (lo + wide) // LANES, :] = (
+            flat_ref[0, :, lo : lo + wide].astype(f32).reshape(wide // LANES, LANES)
+        )
+    pairs, per_pair, tiles = shard_rows // 2, 2 * depth // LANES, -(-depth // LANES)
+    w_wide[...] = jnp.zeros_like(w_wide)
+    lower = lax.broadcasted_iota(jnp.int32, (pairs, LANES), 1) < LANES // 2
+
+    def chunk(j):
+        return chunks_ref[pl.ds(j, pairs, stride=per_pair), :]
+
+    middle = chunk(tiles - 1)
+    for j in range(tiles - 1):
+        w_wide[j, pl.ds(0, pairs, stride=2), :] = chunk(j)
+    w_wide[tiles - 1, pl.ds(0, pairs, stride=2), :] = jnp.where(lower, middle, 0.0)
+    turned = pltpu.roll(middle, LANES // 2, 1)
+    for j in range(tiles):
+        if j + 1 < tiles:
+            following = pltpu.roll(chunk(tiles + j), LANES // 2, 1)
+        else:
+            following = jnp.zeros_like(turned)
+        w_wide[j, pl.ds(1, pairs, stride=2), :] = jnp.where(lower, turned, following)
+        turned = following
+    for j in range(w_wide.shape[0]):
+        w_ref[:, j * LANES : (j + 1) * LANES] = w_wide[j].astype(bf16)
+    for condition, copy in locals_:
+        pl.when(condition)(copy.start)
     swap.wait_recv()
     own[...] = state[b] + unpack(band_in[...])
 
@@ -285,8 +288,13 @@
             hop.start()
 
         sends.append((t + d < n, hop))
-        if s >= hops - 2:
-            forward(1, (s - hops + 2,))
+        if s == 0:
+            first_step(b)
+        elif s == 1:
+            first_step(ob)
+            w_put(own_rows, me_slot, t, ob)
+        elif s == 2:
+            forward(1, (b,))
 
         @pl.when(t >= d)
         def _():
@@ -297,66 +305,73 @@
     swap = remote(final.at[b], final.at[b], s_send.at[1 + hops], s_recv.at[1 + hops], at(y, t, ob))
     swap.start()
     sends.append((None, swap))
+    forward(1, (ob,))
+    arrived += [chip(pos - 1), chip(pos + 1)]
     swap.wait_recv()
 
     loads[3].wait()
     loads[4].wait()
-    total = jnp.zeros((tokens, 1), f32)
-    for g in range(groups):
-        lo, wide = g * LANES, min(LANES, depth - g * LANES)
-        qg = jnp.maximum(q_ref[:, lo : lo + wide], 0)
-        packed = final[g // per_half, :, pl.ds((g % per_half) * LANES, wide)]
-        same = (
-            lax.broadcasted_iota(jnp.int32, (wide, wide), 0) // HD
-            == lax.broadcasted_iota(jnp.int32, (wide, wide), 1) // HD
-        )
-        small = packed.astype(f32)
-        tall = jnp.concatenate([small] * (wide // HD), axis=0)
-        numer = jnp.dot(qg, jnp.where(same, tall, 0.0).astype(bf16), preferred_element_type=f32)
-        sums = final[g // per_half, :, half : half + wide].astype(f32)
-        row = g % per_half
-        weigh = sums[row : row + 1] + sums[rows + row : rows + row + 1]
-        terms = qg.astype(f32) * weigh
-        hi = terms.astype(bf16)
-        rest = (terms - hi.astype(f32)).astype(bf16)
-        block_ones = jnp.where(same, 1.0, 0.0).astype(bf16)
-        denom = (
-            jnp.dot(hi, block_ones, preferred_element_type=f32)
-            + jnp.dot(rest, block_ones, preferred_element_type=f32)
-        )
-        r = numer / (denom + read_epsilon)
-        reads[:, lo : lo + wide] = r
-        total = total + jnp.sum(r * r, axis=-1, keepdims=True)
-    scale = lax.rsqrt(total * (1.0 / depth) + norm_epsilon)
-    normed = reads[...] * scale * g_ref[...][None, :]
+    partner_slot, far_slot, far_partner = y * 2 + ob, oy * 2 + b, oy * 2 + ob
     shards, few = 2 * n, shard_rows - main
-    gap = jnp.zeros((tokens, wrest.shape[1] - few), f32)
-    extra = []
-    for j in range(shards):
-        slot, lo = 2 * (j % n) + j // n, j * shard_rows
-        abuf[mine, :, slot * main : (slot + 1) * main] = normed[:, lo : lo + main].astype(bf16)
-    for slot in range(shards):
-        lo = (slot % 2 * n + slot // 2) * shard_rows + main
-        extra += [normed[:, lo : lo + few], gap]
-    abuf[mine, :, shards * main :] = jnp.concatenate(extra, axis=1).astype(bf16)
-
-    partner_slot, far_slot, far_partner = y * 2 + ob, oy * 2 + b, oy * 2 + ob
-
-    def a_put(slot, i, peer):
-        copy = remote(abuf.at[slot], abuf.at[slot], a_send.at[i], a_recv.at[slot], peer)
+    part = tokens // 2
+
+    def piece(slot, h):
+        return abuf.at[slot, pl.ds(h * part, part), :]
+
+    def a_put(slot, h, i, peer):
+        view = piece(slot, h)
+        copy = remote(view, view, a_send.at[i, h], a_recv.at[slot, h], peer)
         copy.start()
         sends.append((None, copy))
 
-    def a_wait(slot):
-        remote(abuf.at[slot], abuf.at[slot], a_send.at[0], a_recv.at[slot], at(y, t, ob)).wait_recv()
-
-    a_put(mine, 0, at(oy, t, b))
-    a_put(mine, 1, at(y, t, ob))
+    def a_wait(slot, h):
+        view = piece(slot, h)
+        remote(view, view, a_send.at[0, h], a_recv.at[slot, h], at(y, t, ob)).wait_recv()
+
+    for h in range(2):
+        top = h * part
+        total = jnp.zeros((part, 1), f32)
+        for g in range(groups):
+            lo, wide = g * LANES, min(LANES, depth - g * LANES)
+            row = g % per_half
+            qg = jnp.maximum(q_ref[top : top + part, lo : lo + wide], 0)
+            small = final[g // per_half, :, pl.ds(row * LANES, wide)].astype(f32)
+            same = (
+                lax.broadcasted_iota(jnp.int32, (wide, wide), 0) // HD
+                == lax.broadcasted_iota(jnp.int32, (wide, wide), 1) // HD
+            )
+            tall = jnp.concatenate([small] * (wide // HD), axis=0)
+            numer = jnp.dot(qg, jnp.where(same, tall, 0.0).astype(bf16), preferred_element_type=f32)
+            sums = final[g // per_half, :, half : half + wide].astype(f32)
+            weigh = sums[row : row + 1] + sums[rows + row : rows + row + 1]
+            terms = qg.astype(f32) * weigh
+            hi = terms.astype(bf16)
+            rest = (terms - hi.astype(f32)).astype(bf16)
+            block_ones = jnp.where(same, 1.0, 0.0).astype(bf16)
+            both = jnp.concatenate([hi, rest], axis=0)
+            denom = jnp.dot(both, block_ones, preferred_element_type=f32)
+            r = numer / (denom[:part] + denom[part:] + read_epsilon)
+            reads[top : top + part, lo : lo + wide] = r
+            total = total + jnp.sum(r * r, axis=-1, keepdims=True)
+        scale = lax.rsqrt(total * (1.0 / depth) + norm_epsilon)
+        normed = reads[top : top + part, :] * scale * g_ref[...][None, :]
+        gap = jnp.zeros((part, wrest.shape[1] - few), f32)
+        extra = []
+        for slot in range(shards):
+            lo = (slot % 2 * n + slot // 2) * shard_rows
+            abuf[mine, top : top + part, slot * main : (slot + 1) * main] = normed[
+                :, lo : lo + main
+            ].astype(bf16)
+            extra += [normed[:, lo + main : lo + shard_rows], gap]
+        abuf[mine, top : top + part, shards * main :] = jnp.concatenate(extra, axis=1).astype(bf16)
+        a_put(mine, h, 0, at(oy, t, b))
+        a_put(mine, h, 1, at(y, t, ob))
 
     if n > 4:
         forward(2)
     acc[...] = jnp.zeros_like(acc)
-    a_wait(partner_slot)
+    for h in range(2):
+        a_wait(partner_slot, h)
     for s in range(3, n // 2):
         forward(s)
     for condition, copy in locals_:
@@ -377,9 +392,11 @@
 
     for p in arrived:
         add(p, y)
-    a_wait(far_slot)
-    a_put(far_slot, 2, at(y, t, ob))
-    a_wait(far_partner)
+    for h in range(2):
+        a_wait(far_slot, h)
+        a_put(far_slot, h, 2, at(y, t, ob))
+    for h in range(2):
+        a_wait(far_partner, h)
     for p in arrived:
         add(p, oy)
     arrived.clear()
@@ -474,8 +491,8 @@
             dma((2 * n,)),
             dma((hops + 2,)),
             dma((hops + 2,)),
-            dma((3,)),
-            dma((4,)),
+            dma((3, 2)),
+            dma((4, 2)),
             dma((3,)),
             dma((4,)),
         ],
@@ -491,7 +508,7 @@
 
     def body(query_tokens, key_tokens, value_tokens, norm_gain, out_weight):
         depth = query_tokens.shape[3]
-        ring = n >= 4 and n & (n - 1) == 0 and bands == 2 and parts == 2
+        ring = n >= 8 and n & (n - 1) == 0 and bands == 2 and parts == 2
         whole_pairs = out_weight.size % (2 * depth) == 0 and depth % LANES == LANES // 2
         few = round_up(-(-depth // 2), LANES) // LANES <= HD // 2
         ring = ring and LANES < out_weight.size // depth

time: 56.9 us -> 52.4 us (0.921)
  the two profiles are of different devices: /device:TPU:29 before, /device:TPU:31 now
where the time goes in v5:
time: 52.4 us; the launch traced here: 51.5 us
  Pallas kernels  49.5 us (94%)
  local copies, waits for them, and re-layouts  1.92 us (4%)
    pallas_call x1, Pallas kernels, fast_body(): pl.pallas_call(functools.partial(kernel, n, shard_rows), out_shape=jax.Sh...  49.5 us
    unnamed x1, local copies, waits for them, and re-layouts  1.92 us

profile of v5, /device:TPU:31, one launch (start us, length us, event | category | flops | bytes accessed | tf_op | source)
XLA Modules:
  0.0 51.5 jit_solution(17881264740456422538)
XLA Ops:
  0.0 49.5 %shard_map.55 = bf16[128,2240]{1,0:T(8,128)(2,1)} custom-call(bf16[128,2240]{1,0:T(8,128)(2,1)} %bitcast.5, bf16[128,2240]{1,0:T(8,128)(2,1)} %bitcast.6, bf16[128,2240]{1,0:T(8,128)(2,1)} %bitcast.7, f32[2240]{0:T(1024)} %g_hbm.1, bf16[1,1,313600]{2,1,0:T(2,128)(2,1)} %flat_hbm.1), custom_call_target="tpu_custom_call" | custom-call | tf_op jit(solution)/shard_map/pallas_call | solution.py:460
  49.6 1.9 %copy.7 = bf16[1,4,32,2240]{3,2,1,0:T(8,128)(2,1)} copy(bf16[1,4,32,2240]{3,2,1,0:T(8,128)(2,1)} %bitcast.4) | data formatting | bytes 1146880

commit v6 on v5

--- a/solution.py
+++ b/solution.py
@@ -366,14 +366,10 @@
         abuf[mine, top : top + part, shards * main :] = jnp.concatenate(extra, axis=1).astype(bf16)
         a_put(mine, h, 0, at(oy, t, b))
         a_put(mine, h, 1, at(y, t, ob))
-
-    if n > 4:
-        forward(2)
+        forward(2, ((b, ob)[h],))
+
+    arrived += [chip(pos - 2), chip(pos + 2)]
     acc[...] = jnp.zeros_like(acc)
-    for h in range(2):
-        a_wait(partner_slot, h)
-    for s in range(3, n // 2):
-        forward(s)
     for condition, copy in locals_:
         pl.when(condition)(copy.wait)
     w_wait(2 * t + ob)
@@ -390,11 +386,18 @@
         rows = wrest[...].reshape(-1, block)
         acc[side] += jnp.dot(both, rows, preferred_element_type=f32)
 
+    for h in range(2):
+        a_wait(partner_slot, h)
+    early = len(arrived)
     for p in arrived:
         add(p, y)
+    for s in range(3, n // 2):
+        forward(s)
     for h in range(2):
         a_wait(far_slot, h)
         a_put(far_slot, h, 2, at(y, t, ob))
+    for p in arrived[early:]:
+        add(p, y)
     for h in range(2):
         a_wait(far_partner, h)
     for p in arrived:

time: 52.4 us -> 51.6 us (0.985); the launches traced: 51.5 us -> 51.5 us
  no operation moved by 1% of the time
where the time goes in v6:
time: 51.6 us; the launch traced here: 51.5 us
  Pallas kernels  49.6 us (96%)
  local copies, waits for them, and re-layouts  1.92 us (4%)
    pallas_call x1, Pallas kernels, fast_body(): pl.pallas_call(functools.partial(kernel, n, shard_rows), out_shape=jax.Sh...  49.6 us
    unnamed x1, local copies, waits for them, and re-layouts  1.92 us

profile of v6, /device:TPU:31, one launch (start us, length us, event | category | flops | bytes accessed | tf_op | source)
XLA Modules:
  0.0 51.5 jit_solution(13457690463541951444)
XLA Ops:
  0.0 49.6 %shard_map.55 = bf16[128,2240]{1,0:T(8,128)(2,1)} custom-call(bf16[128,2240]{1,0:T(8,128)(2,1)} %bitcast.5, bf16[128,2240]{1,0:T(8,128)(2,1)} %bitcast.6, bf16[128,2240]{1,0:T(8,128)(2,1)} %bitcast.7, f32[2240]{0:T(1024)} %g_hbm.1, bf16[1,1,313600]{2,1,0:T(2,128)(2,1)} %flat_hbm.1), custom_call_target="tpu_custom_call" | custom-call | tf_op jit(solution)/shard_map/pallas_call | solution.py:463
  49.6 1.9 %copy.7 = bf16[1,4,32,2240]{3,2,1,0:T(8,128)(2,1)} copy(bf16[1,4,32,2240]{3,2,1,0:T(8,128)(2,1)} %bitcast.4) | data formatting | bytes 1146880
